TPU v7x, 32 devices: a whole 2x2x4 slice. The times are simulated.
32 devices in a mesh: leaf: 8 (over z, y), panel: 4 (over x, core).
Axes of the slice: x: 2, y: 2, z: 4, core: 2. Of those that a mesh axis runs over, the one named last changes fastest.
Arguments:
- subtree_solution: bfloat16 [32, 4, 16384], P(None, 'panel', 'leaf'), may hold values from -6 to 6
- subtree_coupling: bfloat16 [4, 1024, 2048], P('panel', 'leaf'), may hold values from -0.25 to 0.25
- sub_map: int32 [4, 1024], P('panel', 'leaf'), may hold values from 0 to 8191
- sub_count: int32 [4, 8], P('panel', 'leaf'), may hold values from 1 to 128, 512 in all within a row
- front_rhs: float32 [32, 4, 8192], P(None, 'panel', 'leaf'), may hold values from -6 to 6
- sep_inverse: bfloat16 [4, 8192, 8192], P('panel', None, 'leaf'), may hold values from -0.0625 to 0.0625
- border_coupling: bfloat16 [4, 8192, 2048], P('panel', 'leaf'), may hold values from -0.0625 to 0.0625
- border_map: int32 [4, 2048], replicated, may hold values from 0 to 10239
- root_rhs: float32 [32, 10240], P(None, 'panel'), may hold values from -6 to 6
- root_inverse: bfloat16 [10240, 10240], P('leaf', 'panel'), may hold values from -0.0625 to 0.0625
Outputs:
- root_forward: float32 [32, 10240], P(None, 'leaf')
- root_solution: float32 [32, 10240], P(None, 'panel')
- front_solution: float32 [32, 4, 8192], P(None, 'panel', 'leaf')
- subtree_update: float32 [32, 4, 16384], P(None, 'panel', 'leaf')
Inputs may be any that keep to these rules, and one draw needn't show every extreme that they name: `sub_map`: only the first sub_count entries of a subtree's rows are live. `sub_count`: over one front's 8 subtrees the counts sum to 512.
All inputs are finite; a program needn't handle non-finite values. No bound on the sum of `sub_count` on one device may be relied on, other than what follows from the above.
Results may differ from a plain program's by a relative error of at most 0.0075.
Values may be sent and summed in bfloat16 or wider, within the bound.
A program may use at most 64 MiB of HBM per device.

v0:
```python
import jax
import jax.numpy as jnp
from jax import lax
from jax.sharding import PartitionSpec as P


def body(
    subtree_solution,
    subtree_coupling,
    sub_map,
    sub_count,
    front_rhs,
    sep_inverse,
    border_coupling,
    border_map,
    root_rhs,
    root_inverse,
):
    solved_values = subtree_solution[:, 0, :]
    coupling_factor = subtree_coupling[0]
    rows_sub = coupling_factor.shape[0]
    living = jnp.arange(rows_sub, dtype=jnp.int32) < sub_count[0, 0]
    contrib = lax.dot_general(
        solved_values, coupling_factor, (((1,), (1,)), ((), ())), preferred_element_type=jnp.float32
    )
    contrib = jnp.where(living[None, :], contrib, jnp.zeros_like(contrib))
    slab = sep_inverse[0]
    sep_width = slab.shape[0]
    batch = solved_values.shape[0]
    extended = jnp.zeros((batch, sep_width), jnp.float32).at[:, sub_map[0]].add(contrib)
    arrived = lax.psum_scatter(extended, "leaf", scatter_dimension=1, tiled=True)
    assembled = (front_rhs[:, 0, :] - arrived).astype(jnp.bfloat16)
    partial_rows = lax.dot_general(
        assembled, slab, (((1,), (1,)), ((), ())), preferred_element_type=jnp.float32
    )
    forward = lax.psum_scatter(partial_rows, "leaf", scatter_dimension=1, tiled=True)
    border_rows_local = border_coupling[0]
    partial_border = jnp.dot(
        forward.astype(jnp.bfloat16), border_rows_local, preferred_element_type=jnp.float32
    )
    border_term = lax.psum(partial_border, "leaf")
    panel_index = lax.axis_index("panel")
    col_width = root_rhs.shape[1]
    root_width = col_width * lax.axis_size("panel")
    own_map = border_map[panel_index]
    spread = jnp.zeros((batch, root_width), jnp.float32).at[:, own_map].add(border_term)
    root_term = lax.psum_scatter(spread, "panel", scatter_dimension=1, tiled=True)
    root_assembled = (root_rhs - root_term).astype(jnp.bfloat16)
    root_partial = lax.dot_general(
        root_assembled, root_inverse, (((1,), (1,)), ((), ())), preferred_element_type=jnp.float32
    )
    root_forward = lax.psum(root_partial, "panel")
    column_partial = jnp.dot(
        root_forward.astype(jnp.bfloat16), root_inverse, preferred_element_type=jnp.float32
    )
    root_solution = lax.psum(column_partial, "leaf")
    root_half = root_solution.astype(jnp.bfloat16)
    whole_root = lax.all_gather(root_half, "panel", axis=1, tiled=True)
    border_values = whole_root[:, own_map]
    correction = lax.dot_general(
        border_values,
        border_rows_local,
        (((1,), (1,)), ((), ())),
        preferred_element_type=jnp.float32,
    )
    residual = (forward - correction).astype(jnp.bfloat16)
    front_solution = jnp.dot(
        lax.all_gather(residual, "leaf", axis=1, tiled=True),
        slab,
        preferred_element_type=jnp.float32,
    )
    front_half = front_solution.astype(jnp.bfloat16)
    whole_front = lax.all_gather(front_half, "leaf", axis=1, tiled=True)
    picked = whole_front[:, sub_map[0]]
    picked = jnp.where(living[None, :], picked, jnp.zeros_like(picked))
    subtree_update = jnp.dot(picked, coupling_factor, preferred_element_type=jnp.float32)
    return (root_forward, root_solution, front_solution[:, None, :], subtree_update[:, None, :])


def solution(mesh):
    return jax.shard_map(
        body,
        mesh=mesh,
        in_specs=(
            P(None, "panel", "leaf"),
            P("panel", "leaf", None),
            P("panel", "leaf"),
            P("panel", "leaf"),
            P(None, "panel", "leaf"),
            P("panel", None, "leaf"),
            P("panel", "leaf", None),
            P(),
            P(None, "panel"),
            P("leaf", "panel"),
        ),
        out_specs=(
            P(None, "leaf"),
            P(None, "panel"),
            P(None, "panel", "leaf"),
            P(None, "panel", "leaf"),
        ),
        check_vma=False,
    )
```

profile of v0, /device:TPU:0, one launch (start us, length us, event | category | flops | bytes accessed | tf_op | source)
XLA Modules:
  0.0 550.9 jit_solution(6112033320869614807)
XLA Ops:
  7.2 0.0 copy-start
  7.2 0.0 reduce-scatter.4.cloned.1.call-start
  7.9 0.7 fusion.32
  8.6 0.0 copy-done
  8.6 1.2 fusion.18
  9.8 0.0 copy-start.4
  9.8 3.2 scatter_custom_fusion
  13.0 0.0 reduce-scatter.4.cloned.1.call-update
  13.0 0.0 reduce-scatter.6.cloned.1.call-start
  13.0 0.0 copy-done.4
  13.0 0.2 copy.20
  13.3 90.5 %reduce-scatter.4.cloned.1.call-done = f32[32,1024]{0,1:T(8,128)} async-done(((f32[32,8192]{0,1:T(8,128)}), f32[32,1024]{0,1:T(8,128)}) %reduce-scatter.4.cloned.1.call-update) | async-done | bytes 131088 | tf_op jit(solution)/shard_map/reduce_scatter | solution.py:31
  103.7 12.1 %fusion.2 = f32[32,8192]{1,0:T(8,128)} fusion(bf16[1,8192,1024]{2,1,0:T(8,128)(2,1)} %param.15, f32[32,1024]{0,1:T(8,128)} %reduce-scatter.4.cloned.1.call-done, f32[32,1,1024]{0,2,1:T(8,128)S(1)} %copy.20), kind=kOutput, calls=%fused_computation.6 | convolution fusion | flops 536936448 | bytes 18087936 | tf_op jit(solution)/shard_map/dot_general | solution.py:33
  115.8 0.0 reduce-scatter.6.cloned.1.call-update
  115.9 0.0 all-reduce.4.cloned.1.call-start
  115.9 63.6 %reduce-scatter.6.cloned.1.call-done = f32[32,1024]{1,0:T(8,128)} async-done(((f32[32,8192]{1,0:T(8,128)}), f32[32,1024]{1,0:T(8,128)}) %reduce-scatter.6.cloned.1.call-update) | async-done | bytes 131088 | tf_op jit(solution)/shard_map/reduce_scatter | solution.py:36
  179.5 5.0 fusion.6
  184.5 0.0 all-reduce.4.cloned.1.call-update
  184.5 0.0 reduce-scatter.8.cloned.1.call-start
  184.6 0.8 compare_select_fusion
  185.3 76.4 %all-reduce.4.cloned.1.call-done = f32[32,2048]{0,1:T(8,128)} async-done(((f32[32,2048]{0,1:T(8,128)}), f32[32,2048]{0,1:T(8,128)}) %all-reduce.4.cloned.1.call-update) | async-done | bytes 262160 | tf_op jit(solution)/shard_map/psum | solution.py:41
  261.7 13.4 %scatter_custom_fusion.1 = f32[32,10240]{0,1:T(8,128)} fusion(s32[2048]{0:T(1024)S(1)} %bitcast.51, f32[]{:T(128)} %constant.7.clone.1, f32[32,2048]{0,1:T(8,128)} %all-reduce.4.cloned.1.call-done), kind=kCustom, calls=%fused_computation.12 | custom fusion | flops 65536 | bytes 1572868 | tf_op jit(solution)/shard_map/scatter-add | solution.py:46
  275.2 0.0 copy-start.3
  275.2 0.0 reduce-scatter.8.cloned.1.call-update
  275.2 0.0 all-reduce.6.cloned.1.call-start
  275.2 0.9 copy-done.3
  276.1 0.4 copy.21
  276.5 49.8 %reduce-scatter.8.cloned.1.call-done = f32[32,2560]{0,1:T(8,128)} async-done(((f32[32,10240]{0,1:T(8,128)}), f32[32,2560]{0,1:T(8,128)}) %reduce-scatter.8.cloned.1.call-update) | async-done | bytes 327696 | tf_op jit(solution)/shard_map/reduce_scatter | solution.py:47
  326.3 6.0 %fusion.20 = f32[32,1280]{1,0:T(8,128)} fusion(bf16[1280,2560]{1,0:T(8,128)(2,1)} %param.19, f32[32,2560]{0,1:T(8,128)S(1)} %copy.21, f32[32,2560]{0,1:T(8,128)} %reduce-scatter.8.cloned.1.call-done), kind=kOutput, calls=%fused_computation.23 | convolution fusion | flops 209879040 | bytes 7372800 | tf_op jit(solution)/shard_map/dot_general | solution.py:49
  332.3 0.0 all-reduce.6.cloned.1.call-update
  332.3 0.0 all-reduce.8.cloned.1.call-start
  332.4 31.7 %all-reduce.6.cloned.1.call-done = f32[32,1280]{1,0:T(8,128)} async-done(((f32[32,1280]{1,0:T(8,128)}), f32[32,1280]{1,0:T(8,128)}) %all-reduce.6.cloned.1.call-update) | async-done | bytes 163856 | tf_op jit(solution)/shard_map/psum | solution.py:52
  364.0 4.9 fusion.26
  369.0 0.0 copy-start.2
  369.0 0.0 all-reduce.8.cloned.1.call-update
  369.0 71.1 %all-reduce.8.cloned.1.call-done = f32[32,2560]{1,0:T(8,128)} async-done(((f32[32,2560]{1,0:T(8,128)}), f32[32,2560]{1,0:T(8,128)}) %all-reduce.8.cloned.1.call-update) | async-done | bytes 327696 | tf_op jit(solution)/shard_map/psum | solution.py:56
  440.1 1.0 convert_element_type.25
  441.1 8.5 %all_gather.9 = bf16[32,10240]{1,0:T(8,128)(2,1)} all-gather(bf16[32,2560]{1,0:T(8,128)(2,1)S(1)} %convert_element_type.25), channel_id=1, replica_groups=mesh['leaf'=8,'panel'=4] {'panel'}, dimensions={1}, use_global_device_ids=true | all-gather | bytes 819200 | tf_op jit(solution)/shard_map/all_gather | solution.py:58
  449.6 3.3 copy.22
  452.9 8.0 %gather_fusion = bf16[2048,32]{1,0:T(8,128)(2,1)} fusion(bf16[32,10240]{0,1:T(8,128)(2,1)S(1)} %copy.22, s32[2048]{0:T(1024)S(1)} %broadcast_clamp_fusion), kind=kCustom, calls=%fused_computation | custom fusion | bytes 270336 | tf_op jit(solution)/shard_map/gather | solution.py:59
  460.9 0.0 copy-done.2
  460.9 3.7 fusion.15
  464.7 31.6 %all_gather.10 = bf16[32,8192]{1,0:T(8,128)(2,1)S(1)} all-gather(bf16[32,1024]{1,0:T(8,128)(2,1)S(1)} %fusion.15), channel_id=1, replica_groups=mesh['leaf'=8,'panel'=4] {'leaf'}, dimensions={1}, use_global_device_ids=true | all-gather | bytes 589824 | tf_op jit(solution)/shard_map/all_gather | solution.py:68
  496.2 9.4 %fusion.34 = (bf16[32,1024]{1,0:T(8,128)(2,1)S(1)}, f32[32,1024]{1,0:T(8,128)}) fusion(bf16[32,8192]{1,0:T(8,128)(2,1)S(1)} %all_gather.10, bf16[1,8192,1024]{2,1,0:T(8,128)(2,1)} %param.15), kind=kOutput, calls=%fused_computation.42 | convolution fusion | flops 536903680 | bytes 17498112 | tf_op jit(solution)/shard_map/dot_general | solution.py:67
  505.7 0.0 copy-start.1
  505.7 31.3 %all_gather.11 = bf16[32,8192]{1,0:T(8,128)(2,1)S(1)} all-gather(bf16[32,1024]{1,0:T(8,128)(2,1)S(1)} %get-tuple-element.12), channel_id=1, replica_groups=mesh['leaf'=8,'panel'=4] {'leaf'}, dimensions={1}, use_global_device_ids=true | all-gather | bytes 589824 | tf_op jit(solution)/shard_map/all_gather | solution.py:73
  537.0 1.0 copy.23
  538.0 0.7 gather_fusion.1
  538.7 0.3 convolution_bitcast_fusion
  539.0 1.0 copy.25
  540.0 1.7 copy.24
  541.7 1.6 copy.30
  543.3 0.0 copy-done.1
  543.3 0.7 copy.31
  (3 shorter events, 0.0 us)
Async XLA Ops:
  7.2 1.4 copy-start
  7.2 96.6 %reduce-scatter.4.cloned.1.call-start = ((), (), s32[]{:S(2)}) async-start(), calls=%async_computation.3 | async-start | bytes 4718592 | tf_op jit(solution)/shard_map/reduce_scatter | solution.py:31
  9.8 3.3 copy-start.4
  13.0 166.5 %reduce-scatter.6.cloned.1.call-start = ((), (), s32[]{:S(2)}) async-start(), calls=%async_computation.4 | async-start | bytes 1179648 | tf_op jit(solution)/shard_map/reduce_scatter | solution.py:36
  115.9 145.9 %all-reduce.4.cloned.1.call-start = ((), (), s32[]{:S(2)}) async-start(), calls=%async_computation.5 | async-start | bytes 2097152 | tf_op jit(solution)/shard_map/psum | solution.py:41
  184.5 141.8 %reduce-scatter.8.cloned.1.call-start = ((), (), s32[]{:S(2)}) async-start(), calls=%async_computation.6 | async-start | bytes 6553600 | tf_op jit(solution)/shard_map/reduce_scatter | solution.py:47
  275.2 1.0 copy-start.3
  275.2 88.9 %all-reduce.6.cloned.1.call-start = ((), (), s32[]{:S(2)}) async-start(), calls=%async_computation.7 | async-start | bytes 327680 | tf_op jit(solution)/shard_map/psum | solution.py:52
  332.3 107.8 %all-reduce.8.cloned.1.call-start = ((), (), s32[]{:S(2)}) async-start(), calls=%async_computation.8 | async-start | bytes 655360 | tf_op jit(solution)/shard_map/psum | solution.py:56
  369.0 92.0 %copy-start.2 = (f32[32,1024]{1,0:T(8,128)S(1)}, f32[32,1024]{1,0:T(8,128)}, u32[]{:S(2)}) copy-start(f32[32,1024]{1,0:T(8,128)} %reduce-scatter.6.cloned.1.call-done) | copy-start | bytes 393220
  505.7 37.7 %copy-start.1 = (f32[32,2560]{1,0:T(8,128)S(1)}, f32[32,2560]{1,0:T(8,128)}, u32[]{:S(2)}) copy-start(f32[32,2560]{1,0:T(8,128)} %all-reduce.8.cloned.1.call-done) | copy-start | bytes 983044
Sparse Core Ops, SparseCore 0:
  13.1 90.5 reduce-scatter.3
  116.0 63.4 reduce-scatter.5
  184.6 77.0 all-reduce.3
  275.3 50.9 reduce-scatter.7
  332.4 31.5 all-reduce.5
  369.1 70.9 all-reduce.7
where the time goes:
time: 551 us
  waiting for transfers between devices  383 us (70%)
  blocking collectives  71.4 us (13%)
  matrix products  42.6 us (8%)
  local copies, waits for them, and re-layouts  19.6 us (4%)
  other arithmetic  19 us (3%)
  between operations  14.9 us (3%)
    reduce_scatter x1, waiting for transfers between devices, body(): lax.psum_scatter(extended, 'leaf', scatter_dimension=1, tiled=True)  90.5 us
    psum x1, waiting for transfers between devices, body(): border_term = lax.psum(partial_border, 'leaf')  76.4 us
    psum x1, waiting for transfers between devices, body(): root_solution = lax.psum(column_partial, 'leaf')  71.1 us
    reduce_scatter x1, waiting for transfers between devices, body(): lax.psum_scatter(partial_rows, 'leaf', scatter_dimension=1, tiled=True)  63.6 us
    reduce_scatter x1, waiting for transfers between devices, body(): lax.psum_scatter(spread, 'panel', scatter_dimension=1, tiled=True)  49.8 us
    psum x1, waiting for transfers between devices, body(): root_forward = lax.psum(root_partial, 'panel')  31.7 us
    all_gather x1, blocking collectives, body(): lax.all_gather(residual, 'leaf', axis=1, tiled=True)  31.6 us
    all_gather x1, blocking collectives, body(): whole_front = lax.all_gather(front_half, 'leaf', axis=1, tiled=True)  31.3 us
  transfers between devices with their start and end apart: 6, of which 6 were waited for; matrix products, arithmetic and copies ran while one was open for 0% of the time, Pallas kernels for 0%

commit v1 on v0

--- a/solution.py
+++ b/solution.py
@@ -1,7 +1,356 @@
+import functools
 import jax
 import jax.numpy as jnp
 from jax import lax
+from jax.experimental import pallas as pl
+from jax.experimental.pallas import tpu as pltpu
 from jax.sharding import PartitionSpec as P
+
+MESH = pl.DeviceIdType.MESH
+BF = jnp.bfloat16
+F32 = jnp.float32
+LANES = 128
+VMEM_BYTES = 56 * 1024 * 1024
+(CON, MAP, FWD, BOR, BPAN, RRS, RAG, RFP, SRS, SAG, PPAN, PAG, RES, PICK) = range(14)
+PANEL_PHASES = (BPAN, RFP, PPAN)
+
+
+def nn(a, b):
+    return jnp.dot(a, b, preferred_element_type=F32)
+
+
+def nt(a, b):
+    return lax.dot_general(a, b, (((1,), (1,)), ((), ())), preferred_element_type=F32)
+
+
+def ceil_to(value, step):
+    return -(-value // step) * step
+
+
+def kernel(
+    n_leaf, n_panel,
+    ss_ref, sc_ref, map_ref, count_ref, rhs_ref, bmap_ref, root_rhs_ref,
+    slab_hbm, border_hbm, root_hbm,
+    rf_out, rs_out, fs_out, su_out,
+    slab, border, root, oh_sub, oh_root, rhs_pad, forward, picks_send,
+    con_l, map_l, fwd_s, fwd_l, bor_s, bor_l, bpan_l, rrs_s, rrs_l, rag_l,
+    rfp_l, srs_s, srs_l, sag_l, ppan_s, ppan_l, pag_l, res_l, pick_l,
+    load_sem, send_sem, recv_sem,
+):
+    leaf = lax.axis_index("leaf")
+    panel = lax.axis_index("panel")
+    batch = ss_ref.shape[0]
+    own = rhs_ref.shape[1]
+    eblk = bor_l.shape[2]
+    blk = rrs_l.shape[2]
+    cols = root_rhs_ref.shape[1]
+    rows_sub = sc_ref.shape[0]
+
+    loads = [
+        pltpu.make_async_copy(slab_hbm, slab, load_sem.at[0]),
+        pltpu.make_async_copy(border_hbm, border, load_sem.at[1]),
+        pltpu.make_async_copy(root_hbm, root, load_sem.at[2]),
+    ]
+    for load in loads:
+        load.start()
+
+    barrier = pltpu.get_barrier_semaphore()
+    for d in range(1, n_leaf):
+        pl.semaphore_signal(
+            barrier, inc=1, device_id=(lax.rem(leaf + d, n_leaf), panel), device_id_type=MESH
+        )
+    for d in range(1, n_panel):
+        pl.semaphore_signal(
+            barrier, inc=1, device_id=(leaf, lax.rem(panel + d, n_panel)), device_id_type=MESH
+        )
+
+    def copy(phase, src, dst, peer):
+        on_panel = phase in PANEL_PHASES
+        me = panel if on_panel else leaf
+        target = (leaf, peer) if on_panel else (peer, panel)
+        return pltpu.make_async_remote_copy(
+            src_ref=src, dst_ref=dst.at[me],
+            send_sem=send_sem.at[phase, peer], recv_sem=recv_sem.at[phase, me],
+            device_id=target, device_id_type=MESH,
+        )
+
+    def group(phase):
+        return (panel, n_panel) if phase in PANEL_PHASES else (leaf, n_leaf)
+
+    def send_all(phase, source, dst):
+        me, n = group(phase)
+
+        def step(d, carry):
+            peer = lax.rem(me + d, n)
+            copy(phase, source(peer), dst, peer).start()
+            return carry
+
+        lax.fori_loop(1, n, step, 0)
+
+    def arrived(phase, dst, source):
+        pltpu.make_async_copy(dst.at[source], dst.at[source], recv_sem.at[phase, source]).wait()
+
+    def arrive_all(phase, dst):
+        me, n = group(phase)
+
+        def step(d, carry):
+            arrived(phase, dst, lax.rem(me - d + n, n))
+            return carry
+
+        lax.fori_loop(1, n, step, 0)
+
+    def sent_all(phase, dst):
+        me, n = group(phase)
+
+        def step(d, carry):
+            peer = lax.rem(me + d, n)
+            pltpu.make_async_copy(dst.at[me], dst.at[me], send_sem.at[phase, peer]).wait()
+            return carry
+
+        lax.fori_loop(1, n, step, 0)
+
+    def total(dst):
+        result = dst[0].astype(F32)
+        for s in range(1, dst.shape[0]):
+            result = result + dst[s].astype(F32)
+        return result
+
+    def joined(dst):
+        return jnp.concatenate([dst[s] for s in range(dst.shape[0])], axis=1)
+
+    def spread_blocks(dst, value):
+        for s in range(n_leaf):
+            width = max(0, min(blk, cols - s * blk))
+            if width:
+                dst[s, :, :width] = value[:, s * blk:s * blk + width].astype(dst.dtype)
+            if width < blk:
+                dst[s, :, width:] = jnp.zeros((batch, blk - width), dst.dtype)
+
+    map_l[leaf] = jnp.broadcast_to(map_ref[...], map_l.shape[1:])
+    contrib = nt(ss_ref[...], sc_ref[...])
+    living = lax.broadcasted_iota(jnp.int32, (batch, rows_sub), 1) < count_ref[0, 0]
+    contrib = jnp.where(living, contrib, 0.0)
+    high = contrib.astype(BF)
+    con_l[leaf, :batch] = high
+    con_l[leaf, batch:] = (contrib - high.astype(F32)).astype(BF)
+
+    pl.semaphore_wait(barrier, n_leaf - 1 + n_panel - 1)
+    send_all(MAP, lambda peer: map_l.at[leaf], map_l)
+    send_all(CON, lambda peer: con_l.at[leaf], con_l)
+
+    spread_blocks(rhs_pad, root_rhs_ref[...])
+    for f in range(n_panel):
+        row = bmap_ref[f:f + 1, pl.ds(pl.multiple_of(leaf * eblk, LANES), eblk)]
+
+        def mark_root(c, carry, f=f, row=row):
+            at = pl.multiple_of(c * LANES, LANES)
+            column = lax.broadcasted_iota(jnp.int32, (LANES, eblk), 0) + (panel * cols + at)
+            oh_root[pl.ds(at, LANES), f * eblk:(f + 1) * eblk] = jnp.where(
+                column == row, 1.0, 0.0
+            ).astype(BF)
+            return carry
+
+        lax.fori_loop(0, cols // LANES, mark_root, 0)
+
+    arrive_all(MAP, map_l)
+
+    for s in range(n_leaf):
+        def mark_sub(c, carry, s=s):
+            at = pl.multiple_of(c * LANES, LANES)
+            column = lax.broadcasted_iota(jnp.int32, (LANES, rows_sub), 0) + (leaf * own + at)
+            oh_sub[pl.ds(at, LANES), s * rows_sub:(s + 1) * rows_sub] = jnp.where(
+                column == map_l[s, 0:1, :], 1.0, 0.0
+            ).astype(BF)
+            return carry
+
+        lax.fori_loop(0, own // LANES, mark_sub, 0)
+
+    arrive_all(CON, con_l)
+    both = nt(joined(con_l), oh_sub[...])
+    assembled = (rhs_ref[...] - (both[:batch] + both[batch:])).astype(BF)
+
+    loads[0].wait()
+
+    def forward_step(d, carry):
+        peer = lax.rem(leaf + d, n_leaf)
+        rows = slab[pl.ds(pl.multiple_of(peer * own, LANES), own), :]
+        fwd_s[peer] = nt(assembled, rows).astype(BF)
+        copy(FWD, fwd_s.at[peer], fwd_l, peer).start()
+        return carry
+
+    lax.fori_loop(1, n_leaf, forward_step, 0)
+    mine = nt(assembled, slab[pl.ds(pl.multiple_of(leaf * own, LANES), own), :])
+    fwd_l[leaf] = jnp.zeros((batch, own), BF)
+    arrive_all(FWD, fwd_l)
+    fwd = mine + total(fwd_l)
+    forward[...] = fwd
+    fwd_half = fwd.astype(BF)
+
+    loads[1].wait()
+
+    def border_step(d, carry):
+        peer = lax.rem(leaf + d, n_leaf)
+        part = nn(fwd_half, border[:, pl.ds(pl.multiple_of(peer * eblk, LANES), eblk)])
+        bor_s[peer] = part.astype(BF)
+        copy(BOR, bor_s.at[peer], bor_l, peer).start()
+        return carry
+
+    lax.fori_loop(1, n_leaf, border_step, 0)
+    own_border = nn(fwd_half, border[:, pl.ds(pl.multiple_of(leaf * eblk, LANES), eblk)])
+    bor_l[leaf] = jnp.zeros((batch, eblk), BF)
+    arrive_all(BOR, bor_l)
+    bpan_l[panel] = (own_border + total(bor_l)).astype(BF)
+    send_all(BPAN, lambda peer: bpan_l.at[panel], bpan_l)
+    arrive_all(BPAN, bpan_l)
+
+    spread_blocks(rrs_s, nt(joined(bpan_l), oh_root[...]))
+    send_all(RRS, lambda peer: rrs_s.at[peer], rrs_l)
+    rrs_l[leaf] = rrs_s[leaf]
+    arrive_all(RRS, rrs_l)
+    rag_l[leaf] = (rhs_pad[leaf] - total(rrs_l)).astype(BF)
+    send_all(RAG, lambda peer: rag_l.at[leaf], rag_l)
+    loads[2].wait()
+    arrive_all(RAG, rag_l)
+
+    rfp_l[panel] = nt(joined(rag_l)[:, :cols], root[...]).astype(BF)
+    send_all(RFP, lambda peer: rfp_l.at[panel], rfp_l)
+    arrive_all(RFP, rfp_l)
+    root_forward = total(rfp_l)
+    rf_out[...] = root_forward
+    spread_blocks(srs_s, nn(root_forward.astype(BF), root[...]))
+    send_all(SRS, lambda peer: srs_s.at[peer], srs_l)
+    srs_l[leaf] = srs_s[leaf]
+    arrive_all(SRS, srs_l)
+    sag_l[leaf] = total(srs_l).astype(BF)
+    send_all(SAG, lambda peer: sag_l.at[leaf], sag_l)
+    arrive_all(SAG, sag_l)
+    root_half = joined(sag_l)[:, :cols]
+    rs_out[...] = root_half.astype(F32)
+
+    values = nn(root_half, oh_root[...]).astype(BF)
+    for f in range(n_panel):
+        ppan_s[f] = values[:, f * eblk:(f + 1) * eblk]
+    send_all(PPAN, lambda peer: ppan_s.at[peer], ppan_l)
+    ppan_l[panel] = ppan_s[panel]
+    arrive_all(PPAN, ppan_l)
+    pag_l[leaf] = total(ppan_l).astype(BF)
+    send_all(PAG, lambda peer: pag_l.at[leaf], pag_l)
+    arrive_all(PAG, pag_l)
+
+    residual = forward[...] - nt(joined(pag_l), border[...])
+    res_l[leaf] = residual.astype(BF)
+    send_all(RES, lambda peer: res_l.at[leaf], res_l)
+    fs_out[...] = nn(res_l[leaf], slab[pl.ds(pl.multiple_of(leaf * own, LANES), own), :])
+
+    def back_step(d, carry):
+        source = lax.rem(leaf - d + n_leaf, n_leaf)
+        arrived(RES, res_l, source)
+        fs_out[...] += nn(res_l[source], slab[pl.ds(pl.multiple_of(source * own, LANES), own), :])
+        return carry
+
+    lax.fori_loop(1, n_leaf, back_step, 0)
+
+    picks = nn(fs_out[...].astype(BF), oh_sub[...]).astype(BF)
+    for s in range(n_leaf):
+        picks_send[s] = picks[:, s * rows_sub:(s + 1) * rows_sub]
+    send_all(PICK, lambda peer: picks_send.at[peer], pick_l)
+    pick_l[leaf] = picks_send[leaf]
+    arrive_all(PICK, pick_l)
+    picked = jnp.where(living, total(pick_l), 0.0).astype(BF)
+    su_out[...] = nn(picked, sc_ref[...])
+
+    for phase, dst in (
+        (MAP, map_l), (CON, con_l), (FWD, fwd_l), (BOR, bor_l), (BPAN, bpan_l), (RRS, rrs_l),
+        (RAG, rag_l), (RFP, rfp_l), (SRS, srs_l), (SAG, sag_l), (PPAN, ppan_l), (PAG, pag_l),
+        (RES, res_l), (PICK, pick_l),
+    ):
+        sent_all(phase, dst)
+
+
+def fused(
+    subtree_solution, subtree_coupling, sub_map, sub_count, front_rhs,
+    sep_inverse, border_coupling, border_map, root_rhs, root_inverse,
+):
+    n_leaf, n_panel = lax.axis_size("leaf"), lax.axis_size("panel")
+    batch = subtree_solution.shape[0]
+    rows_sub, top = subtree_coupling.shape[1:]
+    _, sep_width, own = sep_inverse.shape
+    e_width = border_coupling.shape[2]
+    eblk = e_width // n_leaf
+    root_rows, cols = root_inverse.shape
+    blk = ceil_to(-(-cols // n_leaf), LANES)
+    vmem = pl.BlockSpec(memory_space=pltpu.VMEM)
+    anywhere = pl.BlockSpec(memory_space=pl.ANY)
+    smem = pl.BlockSpec(memory_space=pltpu.SMEM)
+
+    def slots(n, width, dtype=BF, rows=batch):
+        return pltpu.VMEM((n, rows, width), dtype)
+
+    results = pl.pallas_call(
+        functools.partial(kernel, n_leaf, n_panel),
+        out_shape=(
+            jax.ShapeDtypeStruct((batch, root_rows), F32),
+            jax.ShapeDtypeStruct((batch, cols), F32),
+            jax.ShapeDtypeStruct((batch, own), F32),
+            jax.ShapeDtypeStruct((batch, top), F32),
+        ),
+        in_specs=[vmem, vmem, vmem, smem, vmem, vmem, vmem, anywhere, anywhere, anywhere],
+        out_specs=(vmem,) * 4,
+        scratch_shapes=[
+            pltpu.VMEM((sep_width, own), BF),
+            pltpu.VMEM((own, e_width), BF),
+            pltpu.VMEM((root_rows, cols), BF),
+            pltpu.VMEM((own, n_leaf * rows_sub), BF),
+            pltpu.VMEM((cols, n_panel * eblk), BF),
+            slots(n_leaf, blk, F32),
+            pltpu.VMEM((batch, own), F32),
+            slots(n_leaf, rows_sub),
+            slots(n_leaf, rows_sub, BF, 2 * batch),
+            slots(n_leaf, rows_sub, jnp.int32, 8),
+            slots(n_leaf, own), slots(n_leaf, own),
+            slots(n_leaf, eblk), slots(n_leaf, eblk),
+            slots(n_panel, eblk),
+            slots(n_leaf, blk), slots(n_leaf, blk), slots(n_leaf, blk),
+            slots(n_panel, root_rows),
+            slots(n_leaf, blk), slots(n_leaf, blk), slots(n_leaf, blk),
+            slots(n_panel, eblk), slots(n_panel, eblk),
+            slots(n_leaf, eblk),
+            slots(n_leaf, own),
+            slots(n_leaf, rows_sub),
+            pltpu.SemaphoreType.DMA((3,)),
+            pltpu.SemaphoreType.DMA((14, max(n_leaf, n_panel))),
+            pltpu.SemaphoreType.DMA((14, max(n_leaf, n_panel))),
+        ],
+        compiler_params=pltpu.CompilerParams(
+            collective_id=0, has_side_effects=True, vmem_limit_bytes=VMEM_BYTES
+        ),
+    )(
+        subtree_solution[:, 0, :], subtree_coupling[0], sub_map, sub_count, front_rhs[:, 0, :],
+        border_map, root_rhs, sep_inverse[0], border_coupling[0], root_inverse,
+    )
+    root_forward, root_solution, front_solution, update = results
+    return root_forward, root_solution, front_solution[:, None, :], update[:, None, :]
+
+
+def fits(
+    subtree_solution, subtree_coupling, sub_map, sub_count, front_rhs,
+    sep_inverse, border_coupling, border_map, root_rhs, root_inverse,
+):
+    n_leaf = lax.axis_size("leaf")
+    widths = (
+        subtree_coupling.shape[1], subtree_coupling.shape[2], sep_inverse.shape[2],
+        border_coupling.shape[2] // n_leaf, root_inverse.shape[0], root_inverse.shape[1],
+    )
+    small = (sep_inverse.size + border_coupling.size + root_inverse.size) * 2 < VMEM_BYTES * 6 // 10
+    return (
+        all(width % LANES == 0 for width in widths)
+        and subtree_solution.shape[0] % 16 == 0
+        and small
+    )
+
+
+def program(*args):
+    return fused(*args) if fits(*args) else body(*args)
 
 
 def body(
@@ -79,7 +428,7 @@
 
 def solution(mesh):
     return jax.shard_map(
-        body,
+        program,
         mesh=mesh,
         in_specs=(
             P(None, "panel", "leaf"),

time: 551 us -> 113 us (0.21)
  waiting for transfers between devices: 383 us -> 0 us
  Pallas kernels: 0 us -> 103 us
  blocking collectives: 71.4 us -> 0 us
  matrix products: 42.6 us -> 0 us
  other arithmetic: 19 us -> 0 us
  between operations: 14.9 us -> 1.29 us
  local copies, waits for them, and re-layouts: 19.6 us -> 8.51 us
    reduce_scatter x3 -> x0, waiting for transfers between devices: 204 us -> none  [the longest x1 90.5 us: body(): lax.psum_scatter(extended, 'leaf', scatter_dimension=1, tiled=True)]
    psum x3 -> x0, waiting for transfers between devices: 179 us -> none  [the longest x1 76.4 us: body(): border_term = lax.psum(partial_border, 'leaf')]
    pallas_call x0 -> x1, Pallas kernels: none -> 103 us  [fused(): pl.pallas_call(functools.partial(kernel, n_leaf, n_panel), out_shape=(jax...]
    all_gather x3 -> x0, blocking collectives: 71.4 us -> none  [the longest x1 31.6 us: body(): lax.all_gather(residual, 'leaf', axis=1, tiled=True)]
    dot_general x8 -> x0, matrix products: 42.6 us -> none  [the longest x1 12.1 us: body(): lax.dot_general(assembled, slab, (((1,), (1,)), ((), ())), preferred_elem...]
    scatter-add x2 -> x0, other arithmetic: 16.6 us -> none  [the longest x1 13.4 us: body(): jnp.zeros((batch, root_width), jnp.float32).at[:, own_map].add(border_term)]
    gather x2 -> x0, local copies, waits for them, and re-layouts: 8.76 us -> none  [the longest x1 8.05 us: body(): border_values = whole_root[:, own_map]]
  transfers between devices with their start and end apart: 6 -> 0, of which waited for: 6 -> 0; matrix products, arithmetic and copies ran while one was open for 0% -> 0% of each run, Pallas kernels for 0% -> 0%
where the time goes in v1:
time: 113 us
  Pallas kernels  103 us (91%)
  local copies, waits for them, and re-layouts  8.51 us (8%)
  between operations  1.29 us (1%)
    pallas_call x1, Pallas kernels, fused(): pl.pallas_call(functools.partial(kernel, n_leaf, n_panel), out_shape=(jax...  103 us
    unnamed x5, local copies, waits for them, and re-layouts  8.51 us

profile of v1, /device:TPU:0, one launch (start us, length us, event | category | flops | bytes accessed | tf_op | source)
XLA Modules:
  0.0 112.9 jit_solution(8057749982963032977)
XLA Ops:
  1.3 1.6 %copy.18 = f32[32,1,1024]{2,0,1:T(8,128)} copy(f32[32,1,1024]{2,1,0:T(1,128)} %param.14) | data formatting | bytes 262144
  2.9 103.1 %shard_map.129 = (f32[32,1280]{1,0:T(8,128)}, f32[32,2560]{1,0:T(8,128)}, f32[32,1024]{1,0:T(8,128)}, f32[32,2048]{1,0:T(8,128)}) custom-call(bf16[32,2048]{1,0:T(8,128)(2,1)} %bitcast.14, bf16[128,2048]{1,0:T(8,128)(2,1)} %bitcast.11, s32[1,128]{1,0:T(1,128)} %map_ref.1, s32[1,1]{1,0:T(1,128)S(6)} %copy.21.count_ref, f32[32,1024]{1,0:T(8,128)} %bitcast.12, ...), custom_call_target="tpu_custom_call" | custom-call | tf_op jit(solution)/shard_map/pallas_call | solution.py:289
  105.9 1.7 %copy.14 = f32[32,1,1024]{2,1,0:T(1,128)} copy(f32[32,1,1024]{2,0,1:T(8,128)} %bitcast.15) | data formatting | bytes 262144
  107.6 1.9 %copy.15 = f32[32,1,2048]{2,1,0:T(1,128)} copy(f32[32,1,2048]{2,0,1:T(8,128)} %bitcast.13) | data formatting | bytes 524288
  109.6 1.6 %copy.22 = f32[32,1280]{1,0:T(8,128)} copy(f32[32,1280]{1,0:T(8,128)} %get-tuple-element.20) | data formatting | bytes 327680
  111.2 1.7 %copy.23 = f32[32,2560]{1,0:T(8,128)} copy(f32[32,2560]{1,0:T(8,128)} %get-tuple-element.21) | data formatting | bytes 655360

commit v2 on v1

--- a/solution.py
+++ b/solution.py
@@ -35,24 +35,27 @@
     slab, border, root, oh_sub, oh_root, rhs_pad, forward, picks_send,
     con_l, map_l, fwd_s, fwd_l, bor_s, bor_l, bpan_l, rrs_s, rrs_l, rag_l,
     rfp_l, srs_s, srs_l, sag_l, ppan_s, ppan_l, pag_l, res_l, pick_l,
-    load_sem, send_sem, recv_sem,
+    slab_sem, load_sem, send_sem, recv_sem,
 ):
     leaf = lax.axis_index("leaf")
     panel = lax.axis_index("panel")
     batch = ss_ref.shape[0]
-    own = rhs_ref.shape[1]
+    own = rhs_ref.shape[2]
     eblk = bor_l.shape[2]
     blk = rrs_l.shape[2]
     cols = root_rhs_ref.shape[1]
     rows_sub = sc_ref.shape[0]
 
+    def slab_load(block):
+        rows = pl.ds(pl.multiple_of(block * own, LANES), own)
+        return pltpu.make_async_copy(slab_hbm.at[rows], slab.at[rows], slab_sem.at[block])
+
     loads = [
-        pltpu.make_async_copy(slab_hbm, slab, load_sem.at[0]),
-        pltpu.make_async_copy(border_hbm, border, load_sem.at[1]),
-        pltpu.make_async_copy(root_hbm, root, load_sem.at[2]),
+        pltpu.make_async_copy(border_hbm, border, load_sem.at[0]),
+        pltpu.make_async_copy(root_hbm, root, load_sem.at[1]),
     ]
-    for load in loads:
-        load.start()
+    for d in range(1, n_leaf + 1):
+        slab_load(lax.rem(leaf + d, n_leaf)).start()
 
     barrier = pltpu.get_barrier_semaphore()
     for d in range(1, n_leaf):
@@ -134,6 +137,7 @@
     con_l[leaf, :batch] = high
     con_l[leaf, batch:] = (contrib - high.astype(F32)).astype(BF)
 
+    forward[...] = rhs_ref[:, 0, :]
     pl.semaphore_wait(barrier, n_leaf - 1 + n_panel - 1)
     send_all(MAP, lambda peer: map_l.at[leaf], map_l)
     send_all(CON, lambda peer: con_l.at[leaf], con_l)
@@ -167,26 +171,30 @@
 
     arrive_all(CON, con_l)
     both = nt(joined(con_l), oh_sub[...])
-    assembled = (rhs_ref[...] - (both[:batch] + both[batch:])).astype(BF)
-
-    loads[0].wait()
+    assembled = (forward[...] - (both[:batch] + both[batch:])).astype(BF)
 
     def forward_step(d, carry):
         peer = lax.rem(leaf + d, n_leaf)
+        slab_load(peer).wait()
         rows = slab[pl.ds(pl.multiple_of(peer * own, LANES), own), :]
         fwd_s[peer] = nt(assembled, rows).astype(BF)
         copy(FWD, fwd_s.at[peer], fwd_l, peer).start()
         return carry
 
     lax.fori_loop(1, n_leaf, forward_step, 0)
+    slab_load(leaf).wait()
+    for load in loads:
+        load.start()
     mine = nt(assembled, slab[pl.ds(pl.multiple_of(leaf * own, LANES), own), :])
     fwd_l[leaf] = jnp.zeros((batch, own), BF)
+    sent_all(MAP, map_l)
+    sent_all(CON, con_l)
     arrive_all(FWD, fwd_l)
     fwd = mine + total(fwd_l)
     forward[...] = fwd
     fwd_half = fwd.astype(BF)
 
-    loads[1].wait()
+    loads[0].wait()
 
     def border_step(d, carry):
         peer = lax.rem(leaf + d, n_leaf)
@@ -198,31 +206,38 @@
     lax.fori_loop(1, n_leaf, border_step, 0)
     own_border = nn(fwd_half, border[:, pl.ds(pl.multiple_of(leaf * eblk, LANES), eblk)])
     bor_l[leaf] = jnp.zeros((batch, eblk), BF)
+    sent_all(FWD, fwd_l)
     arrive_all(BOR, bor_l)
     bpan_l[panel] = (own_border + total(bor_l)).astype(BF)
     send_all(BPAN, lambda peer: bpan_l.at[panel], bpan_l)
+    sent_all(BOR, bor_l)
     arrive_all(BPAN, bpan_l)
 
     spread_blocks(rrs_s, nt(joined(bpan_l), oh_root[...]))
     send_all(RRS, lambda peer: rrs_s.at[peer], rrs_l)
     rrs_l[leaf] = rrs_s[leaf]
+    sent_all(BPAN, bpan_l)
     arrive_all(RRS, rrs_l)
     rag_l[leaf] = (rhs_pad[leaf] - total(rrs_l)).astype(BF)
     send_all(RAG, lambda peer: rag_l.at[leaf], rag_l)
-    loads[2].wait()
+    loads[1].wait()
+    sent_all(RRS, rrs_l)
     arrive_all(RAG, rag_l)
 
     rfp_l[panel] = nt(joined(rag_l)[:, :cols], root[...]).astype(BF)
     send_all(RFP, lambda peer: rfp_l.at[panel], rfp_l)
+    sent_all(RAG, rag_l)
     arrive_all(RFP, rfp_l)
     root_forward = total(rfp_l)
     rf_out[...] = root_forward
     spread_blocks(srs_s, nn(root_forward.astype(BF), root[...]))
     send_all(SRS, lambda peer: srs_s.at[peer], srs_l)
     srs_l[leaf] = srs_s[leaf]
+    sent_all(RFP, rfp_l)
     arrive_all(SRS, srs_l)
     sag_l[leaf] = total(srs_l).astype(BF)
     send_all(SAG, lambda peer: sag_l.at[leaf], sag_l)
+    sent_all(SRS, srs_l)
     arrive_all(SAG, sag_l)
     root_half = joined(sag_l)[:, :cols]
     rs_out[...] = root_half.astype(F32)
@@ -232,14 +247,17 @@
         ppan_s[f] = values[:, f * eblk:(f + 1) * eblk]
     send_all(PPAN, lambda peer: ppan_s.at[peer], ppan_l)
     ppan_l[panel] = ppan_s[panel]
+    sent_all(SAG, sag_l)
     arrive_all(PPAN, ppan_l)
     pag_l[leaf] = total(ppan_l).astype(BF)
     send_all(PAG, lambda peer: pag_l.at[leaf], pag_l)
+    sent_all(PPAN, ppan_l)
     arrive_all(PAG, pag_l)
 
     residual = forward[...] - nt(joined(pag_l), border[...])
     res_l[leaf] = residual.astype(BF)
     send_all(RES, lambda peer: res_l.at[leaf], res_l)
+    sent_all(PAG, pag_l)
     fs_out[...] = nn(res_l[leaf], slab[pl.ds(pl.multiple_of(leaf * own, LANES), own), :])
 
     def back_step(d, carry):
@@ -255,16 +273,18 @@
         picks_send[s] = picks[:, s * rows_sub:(s + 1) * rows_sub]
     send_all(PICK, lambda peer: picks_send.at[peer], pick_l)
     pick_l[leaf] = picks_send[leaf]
+    sent_all(RES, res_l)
     arrive_all(PICK, pick_l)
     picked = jnp.where(living, total(pick_l), 0.0).astype(BF)
     su_out[...] = nn(picked, sc_ref[...])
-
-    for phase, dst in (
-        (MAP, map_l), (CON, con_l), (FWD, fwd_l), (BOR, bor_l), (BPAN, bpan_l), (RRS, rrs_l),
-        (RAG, rag_l), (RFP, rfp_l), (SRS, srs_l), (SAG, sag_l), (PPAN, ppan_l), (PAG, pag_l),
-        (RES, res_l), (PICK, pick_l),
-    ):
-        sent_all(phase, dst)
+    sent_all(PICK, pick_l)
+
+
+def hand_out(rf_ref, rs_ref, fs_ref, su_ref, rf_out, rs_out, fs_out, su_out):
+    rf_out[...] = rf_ref[...]
+    rs_out[...] = rs_ref[...]
+    fs_out[:, 0, :] = fs_ref[...]
+    su_out[:, 0, :] = su_ref[...]
 
 
 def fused(
@@ -317,7 +337,8 @@
             slots(n_leaf, eblk),
             slots(n_leaf, own),
             slots(n_leaf, rows_sub),
-            pltpu.SemaphoreType.DMA((3,)),
+            pltpu.SemaphoreType.DMA((n_leaf,)),
+            pltpu.SemaphoreType.DMA((2,)),
             pltpu.SemaphoreType.DMA((14, max(n_leaf, n_panel))),
             pltpu.SemaphoreType.DMA((14, max(n_leaf, n_panel))),
         ],
@@ -325,11 +346,20 @@
             collective_id=0, has_side_effects=True, vmem_limit_bytes=VMEM_BYTES
         ),
     )(
-        subtree_solution[:, 0, :], subtree_coupling[0], sub_map, sub_count, front_rhs[:, 0, :],
+        subtree_solution[:, 0, :], subtree_coupling[0], sub_map, sub_count, front_rhs,
         border_map, root_rhs, sep_inverse[0], border_coupling[0], root_inverse,
     )
-    root_forward, root_solution, front_solution, update = results
-    return root_forward, root_solution, front_solution[:, None, :], update[:, None, :]
+    return pl.pallas_call(
+        hand_out,
+        out_shape=(
+            jax.ShapeDtypeStruct((batch, root_rows), F32),
+            jax.ShapeDtypeStruct((batch, cols), F32),
+            jax.ShapeDtypeStruct((batch, 1, own), F32),
+            jax.ShapeDtypeStruct((batch, 1, top), F32),
+        ),
+        in_specs=[vmem] * 4,
+        out_specs=(vmem,) * 4,
+    )(*results)
 
 
 def fits(

time: 113 us -> 106 us (0.938)
  local copies, waits for them, and re-layouts: 8.51 us -> 0 us
    unnamed x5 -> x0, local copies, waits for them, and re-layouts: 8.51 us -> none
    pallas_call x0 -> x1, Pallas kernels: none -> 2.12 us  [fused(): pl.pallas_call(hand_out, out_shape=(jax.ShapeDtypeStruct((batch, root_row...]
where the time goes in v2:
time: 106 us; the launch traced here: 105 us
  Pallas kernels  104 us (98%)
  between operations  1.29 us (1%)
    pallas_call x1, Pallas kernels, fused(): pl.pallas_call(functools.partial(kernel, n_leaf, n_panel), out_shape=(jax...  102 us
    pallas_call x1, Pallas kernels, fused(): pl.pallas_call(hand_out, out_shape=(jax.ShapeDtypeStruct((batch, root_row...  2.12 us

profile of v2, /device:TPU:0, one launch (start us, length us, event | category | flops | bytes accessed | tf_op | source)
XLA Modules:
  0.0 105.4 jit_solution(4120498670708252214)
XLA Ops:
  1.3 102.0 %shard_map.129 = (f32[32,1280]{1,0:T(8,128)}, f32[32,2560]{1,0:T(8,128)}, f32[32,1024]{1,0:T(8,128)}, f32[32,2048]{1,0:T(8,128)}) custom-call(bf16[32,2048]{1,0:T(8,128)(2,1)} %bitcast.7, bf16[128,2048]{1,0:T(8,128)(2,1)} %bitcast.6, s32[1,128]{1,0:T(1,128)} %map_ref.1, s32[1,1]{1,0:T(1,128)S(6)} %copy.14.count_ref, f32[32,1,1024]{2,1,0:T(1,128)} %rhs_ref.1, ...), custom_call_target="tpu_custom_call" | custom-call | tf_op jit(solution)/shard_map/pallas_call | solution.py:309
  103.3 2.1 %shard_map.130 = (f32[32,1280]{1,0:T(8,128)}, f32[32,2560]{1,0:T(8,128)}, f32[32,1,1024]{2,1,0:T(1,128)}, f32[32,1,2048]{2,1,0:T(1,128)}) custom-call(f32[32,1280]{1,0:T(8,128)} %get-tuple-element.8.rf_ref, f32[32,2560]{1,0:T(8,128)} %get-tuple-element.9.rs_ref, f32[32,1024]{1,0:T(8,128)} %get-tuple-element.10.fs_ref, f32[32,2048]{1,0:T(8,128)} %get-tuple-element.11.su_ref), custom_call_target="tpu_custom_call" | custom-call | tf_op jit(solution)/shard_map/pallas_call | solution.py:352

commit v3 on v2

--- a/solution.py
+++ b/solution.py
@@ -256,17 +256,44 @@
 
     residual = forward[...] - nt(joined(pag_l), border[...])
     res_l[leaf] = residual.astype(BF)
-    send_all(RES, lambda peer: res_l.at[leaf], res_l)
+    pair = leaf + 1 - 2 * lax.rem(leaf, 2)
+
+    def hand_on(block):
+        return pltpu.make_async_remote_copy(
+            src_ref=res_l.at[block], dst_ref=res_l.at[block],
+            send_sem=send_sem.at[RES, block + 1 - 2 * lax.rem(block, 2)],
+            recv_sem=recv_sem.at[RES, block],
+            device_id=(pair, panel), device_id_type=MESH,
+        )
+
+    def product(block):
+        return nn(res_l[block], slab[pl.ds(pl.multiple_of(block * own, LANES), own), :])
+
+    def direct_step(k, carry):
+        copy(RES, res_l.at[leaf], res_l, lax.rem(leaf + 2 * k, n_leaf)).start()
+        return carry
+
+    lax.fori_loop(1, n_leaf // 2, direct_step, 0)
+    hand_on(leaf).start()
     sent_all(PAG, pag_l)
-    fs_out[...] = nn(res_l[leaf], slab[pl.ds(pl.multiple_of(leaf * own, LANES), own), :])
-
-    def back_step(d, carry):
-        source = lax.rem(leaf - d + n_leaf, n_leaf)
+    fs_out[...] = product(leaf)
+
+    def relay_step(k, carry):
+        source = lax.rem(leaf - 2 * k + n_leaf, n_leaf)
         arrived(RES, res_l, source)
-        fs_out[...] += nn(res_l[source], slab[pl.ds(pl.multiple_of(source * own, LANES), own), :])
+        hand_on(source).start()
+        fs_out[...] += product(source)
         return carry
 
-    lax.fori_loop(1, n_leaf, back_step, 0)
+    lax.fori_loop(1, n_leaf // 2, relay_step, 0)
+
+    def pair_step(k, carry):
+        source = lax.rem(pair - 2 * k + n_leaf, n_leaf)
+        arrived(RES, res_l, source)
+        fs_out[...] += product(source)
+        return carry
+
+    lax.fori_loop(0, n_leaf // 2, pair_step, 0)
 
     picks = nn(fs_out[...].astype(BF), oh_sub[...]).astype(BF)
     for s in range(n_leaf):
@@ -375,6 +402,7 @@
     return (
         all(width % LANES == 0 for width in widths)
         and subtree_solution.shape[0] % 16 == 0
+        and n_leaf % 2 == 0
         and small
     )
 

time: 106 us -> 102 us (0.962)
  Pallas kernels: 104 us -> 101 us
    pallas_call x1, Pallas kernels: 102 us -> 98.6 us  [fused(): pl.pallas_call(functools.partial(kernel, n_leaf, n_panel), out_shape=(jax...]
where the time goes in v3:
time: 102 us
  Pallas kernels  101 us (99%)
  between operations  1.29 us (1%)
    pallas_call x1, Pallas kernels, fused(): pl.pallas_call(functools.partial(kernel, n_leaf, n_panel), out_shape=(jax...  98.6 us
    pallas_call x1, Pallas kernels, fused(): pl.pallas_call(hand_out, out_shape=(jax.ShapeDtypeStruct((batch, root_row...  2.12 us

profile of v3, /device:TPU:0, one launch (start us, length us, event | category | flops | bytes accessed | tf_op | source)
XLA Modules:
  0.0 102.0 jit_solution(12928291748911646772)
XLA Ops:
  1.3 98.6 %shard_map.129 = (f32[32,1280]{1,0:T(8,128)}, f32[32,2560]{1,0:T(8,128)}, f32[32,1024]{1,0:T(8,128)}, f32[32,2048]{1,0:T(8,128)}) custom-call(bf16[32,2048]{1,0:T(8,128)(2,1)} %bitcast.7, bf16[128,2048]{1,0:T(8,128)(2,1)} %bitcast.6, s32[1,128]{1,0:T(1,128)} %map_ref.1, s32[1,1]{1,0:T(1,128)S(6)} %copy.14.count_ref, f32[32,1,1024]{2,1,0:T(1,128)} %rhs_ref.1, ...), custom_call_target="tpu_custom_call" | custom-call | tf_op jit(solution)/shard_map/pallas_call | solution.py:336
  99.9 2.1 %shard_map.130 = (f32[32,1280]{1,0:T(8,128)}, f32[32,2560]{1,0:T(8,128)}, f32[32,1,1024]{2,1,0:T(1,128)}, f32[32,1,2048]{2,1,0:T(1,128)}) custom-call(f32[32,1280]{1,0:T(8,128)} %get-tuple-element.8.rf_ref, f32[32,2560]{1,0:T(8,128)} %get-tuple-element.9.rs_ref, f32[32,1024]{1,0:T(8,128)} %get-tuple-element.10.fs_ref, f32[32,2048]{1,0:T(8,128)} %get-tuple-element.11.su_ref), custom_call_target="tpu_custom_call" | custom-call | tf_op jit(solution)/shard_map/pallas_call | solution.py:379
